TPU v7x, 128 devices: a whole 4x4x4 slice. The times are simulated.
128 devices in a mesh: ctx: 32 (over y, z, core), head: 4 (over x).
Axes of the slice: x: 4, y: 4, z: 4, core: 2. Of those that a mesh axis runs over, the one named last changes fastest.
Arguments:
- queries: bfloat16 [65536, 512], P(('ctx', 'head')), may hold values from -6 to 6
- keys: bfloat16 [65536, 512], P(('ctx', 'head')), may hold values from -6 to 6
- values: bfloat16 [65536, 512], P(('ctx', 'head')), may hold values from -6 to 6
- output: bfloat16 [65536, 512], P(('ctx', 'head')), may hold values from -3 to 3
- out_grad: bfloat16 [65536, 512], P(('ctx', 'head')), may hold values from -6 to 6
- slopes: float32 [4], replicated, may hold values from 4.8828124e-06 to 0.000390625
- windows: int32 [4], replicated, may hold values from 2048 to 6144, as said below
Outputs:
- query_grad: bfloat16 [65536, 512], P(('ctx', 'head'))
- key_grad: bfloat16 [65536, 512], P(('ctx', 'head'))
- value_grad: bfloat16 [65536, 512], P(('ctx', 'head'))
Inputs may be any that keep to these rules, and one draw needn't show every extreme that they name: `windows`: each window is a multiple of 2048; some head has exactly 6144.
All inputs are finite; a program needn't handle non-finite values.
Results may differ from a plain program's by a relative error of at most 0.012.
Values may be sent and summed in bfloat16 or wider, within the bound.
A program may use at most 128 MiB of HBM per device.

v0:
```python
import functools
import math

import jax
import jax.numpy as jnp
from jax import lax
from jax.experimental import pallas as pl
from jax.experimental.pallas import tpu as pltpu
from jax.sharding import PartitionSpec as P

D = 128
SCALE = D ** (-0.5)
LOG2E = math.log2(math.e)
TO_LOG2 = SCALE * LOG2E
BIG = 1e30
F32 = jnp.float32
BF16 = jnp.bfloat16
MESH = pl.DeviceIdType.MESH
SUBS = 4
NT_DIMS = (((1,), (1,)), ((), ()))
TN_DIMS = (((0,), (0,)), ((), ()))

A, B, C, DD = range(4)
QSLOT = (0, 1, 1, 2)
KSLOT = (0, 0, 1, 1)


def kernel(
    n_ctx,
    n_head,
    slopes,
    windows,
    q_in,
    k_in,
    v_in,
    o_in,
    g_in,
    dq_out,
    dk_out,
    dv_out,
    qx,
    kx,
    gb,
    vb,
    ov,
    gv,
    p_ad,
    p_b,
    p_c,
    stat,
    ratio,
    dqt,
    dka,
    dva,
    delta_out,
    delta_in,
    part_out,
    part_in,
    ret_out,
    ret_in,
    dq_send,
    dq_recv,
    dkv_send,
    dkv_recv,
    fin,
    x_ssem,
    x_rsem,
    h_ssem,
    h_rsem,
    d_ssem,
    d_rsem,
    s_ssem,
    s_rsem,
    dq_ssem,
    dq_rsem,
    kv_ssem,
    kv_rsem,
    o_ssem,
    o_rsem,
    l_sem,
):
    ch = q_in.shape[0]
    n = n_head * ch
    sub = ch // SUBS
    ctx = lax.axis_index("ctx")
    me = lax.axis_index("head")
    odd = lax.rem(ctx, 2)
    partner = ctx + 1 - 2 * odd

    def along(by):
        return (lax.rem(ctx + by + n_ctx, n_ctx), me)

    def peer(by):
        return lax.rem(me + by, n_head)

    def rows(j):
        return pl.ds(pl.multiple_of(j * ch, ch), ch)

    def lanes(j):
        return pl.ds(pl.multiple_of(j * D, D), D)

    def remote(src, dst, ssem, rsem, device):
        return pltpu.make_async_remote_copy(
            src_ref=src, dst_ref=dst, send_sem=ssem, recv_sem=rsem,
            device_id=device, device_id_type=MESH,
        )

    sends = []

    def send(src, dst, ssem, rsem, device):
        copy = remote(src, dst, ssem, rsem, device)
        copy.start()
        sends.append(copy)

    def arrived(dst, ssem, rsem):
        remote(dst, dst, ssem, rsem, along(0)).wait_recv()

    slope = slopes[me]
    window = windows[me]

    bufs = (qx, kx, gb, vb)
    ins = (q_in, k_in, g_in, v_in)

    def chunk(a, slot, j):
        if a < 2:
            return bufs[a].at[slot, rows(j), 0:D]
        return bufs[a].at[slot, rows(j), :]

    own = []
    for a in range(4):
        copy = pltpu.make_async_copy(ins[a].at[:, lanes(me)], chunk(a, 0, me), x_rsem.at[a, me])
        copy.start()
        own.append(copy)
    copy_o = pltpu.make_async_copy(o_in, ov, l_sem.at[0])
    copy_g = pltpu.make_async_copy(g_in, gv, l_sem.at[1])
    copy_o.start()
    copy_g.start()

    barrier = pltpu.get_barrier_semaphore()
    neighbours = [along(1), along(-1), along(2), along(-2)]
    neighbours += [(ctx, peer(by)) for by in range(1, n_head)]
    for device in neighbours:
        pl.semaphore_signal(barrier, inc=1, device_id=device, device_id_type=MESH)
    pl.semaphore_wait(barrier, len(neighbours))

    for a in range(4):
        for by in (1, 3, 2):
            to = peer(by)
            send(ins[a].at[:, lanes(to)], chunk(a, 0, me), x_ssem.at[a, by], x_rsem.at[a, me], (ctx, to))

    lane = lax.broadcasted_iota(jnp.int32, (1, D), 1)
    ones = jnp.broadcast_to(jnp.where(lane < 3, 1.0, 0.0), (ch, D)).astype(BF16)

    def fill(t, _):
        for slot in range(3):
            qx[slot, rows(t), D:] = ones
        pos = (lax.broadcasted_iota(jnp.int32, (ch, D), 0) + t * ch).astype(F32)
        bias = pos * (slope / SCALE)
        high = bias.astype(BF16).astype(F32)
        mid = (bias - high).astype(BF16).astype(F32)
        low = bias - high - mid
        terms = jnp.where(lane == 0, high, jnp.where(lane == 1, mid, jnp.where(lane == 2, low, 0.0)))
        for slot in range(2):
            kx[slot, rows(t), D:] = terms.astype(BF16)
        return 0

    lax.fori_loop(0, n_head, fill, 0)

    copy_o.wait()
    copy_g.wait()
    for h in range(n_head):
        prod = gv[:, h * D:(h + 1) * D].astype(F32) * ov[:, h * D:(h + 1) * D].astype(F32)
        sums = jnp.sum(prod.T, axis=0, keepdims=True)
        delta_out[h, :, :] = jnp.broadcast_to(sums, (8, ch))
    keep = pltpu.make_async_copy(delta_out.at[me], delta_in.at[me], d_rsem.at[me])
    keep.start()
    for by in (1, 3, 2):
        to = peer(by)
        send(delta_out.at[to], delta_in.at[me], d_ssem.at[by], d_rsem.at[me], (ctx, to))

    def got_own(a, j):
        arrived(chunk(a, 0, j), x_ssem.at[a, 0], x_rsem.at[a, j])

    def to_partner(a, row, slot, j):
        return remote(
            chunk(a, slot, j), chunk(a, 1, j), h_ssem.at[row, j], h_rsem.at[row, j], (partner, me)
        )

    def forward_rows(a, row, j):
        send(chunk(a, 0, j), chunk(a, 2, j), h_ssem.at[row, j], h_rsem.at[row, j], along(-2))

        @pl.when(odd == 1)
        def _():
            to_partner(a, row + 1, 0, j).start()

    def forward_cols(a, row, j):
        send(chunk(a, 0, j), chunk(a, 1, j), h_ssem.at[row, j], h_rsem.at[row, j], along(1))

    def relay(a, row, j):
        arrived(chunk(a, 2, j), h_ssem.at[row, j], h_rsem.at[row, j])

        @pl.when(odd == 0)
        def _():
            to_partner(a, row + 1, 2, j).start()

        sends.append(to_partner(a, row + 1, 0, j))

    def got_halo(a, row, slot, j):
        arrived(chunk(a, slot, j), h_ssem.at[row, j], h_rsem.at[row, j])

    order_in = (0, 1, 3, 2)

    def store_p(blk, tk, col, width):
        if blk == A:
            return p_ad.at[tk, :, pl.ds(col + ch, width)]
        if blk == DD:
            return p_ad.at[tk, :, pl.ds(col, width)]
        return (p_b if blk == B else p_c).at[tk, :, pl.ds(col, width)]

    def tile_1(blk, tk, col, masked):
        s = lax.dot_general(
            kx[KSLOT[blk], rows(tk), :], qx[QSLOT[blk], pl.ds(col, ch), :], NT_DIMS,
            preferred_element_type=F32,
        )
        if masked:
            apart = lax.broadcasted_iota(jnp.int32, (ch, ch), 1) - lax.broadcasted_iota(
                jnp.int32, (ch, ch), 0
            )
            seen = apart >= 0 if blk == A else apart < window - blk * n
            s = jnp.where(seen, s, -BIG)
        target = store_p(blk, tk, col, ch)
        for u in range(SUBS):
            part = s[u * sub:(u + 1) * sub] * TO_LOG2
            top = jnp.max(part, axis=0, keepdims=True)
            p = jnp.exp2(part - top)
            total = jnp.sum(p, axis=0, keepdims=True)
            target[u * sub:(u + 1) * sub, :] = p.astype(BF16)
            stat[blk * n_head + tk, u:u + 1, pl.ds(col, ch)] = top
            stat[blk * n_head + tk, SUBS + u:SUBS + u + 1, pl.ds(col, ch)] = total

    def phase_1(blk):
        if blk == A:
            for tk in range(n_head):
                for tq in range(tk, n_head):
                    tile_1(blk, tk, tq * ch, tq == tk)
        elif blk == DD:
            for tk in range(n_head):
                for tq in range(tk + 1):
                    tile_1(blk, tk, tq * ch, tq == tk)
        else:
            def body(tk, _):
                for u in range(n_head):
                    tq = lax.rem(tk + u, n_head)
                    tile_1(blk, tk, pl.multiple_of(tq * ch, ch), u == 0)
                return 0

            lax.fori_loop(0, n_head, body, 0)

    exists = (
        None,
        ctx + 1 < n_ctx,
        jnp.logical_and(ctx + 1 < n_ctx, ctx >= 1),
        jnp.logical_and(ctx + 2 < n_ctx, ctx >= 1),
    )
    tq_lane = lax.broadcasted_iota(jnp.int32, (1, n), 1) // ch

    def seen_row(blk, tk):
        if blk == A:
            return tq_lane >= tk
        upto = jnp.where(exists[blk], window - blk * n, -1)
        lower = jnp.logical_and(tq_lane <= tk, upto >= 0)
        upper = jnp.logical_and(tq_lane > tk, upto > 0)
        if blk == DD:
            return lower
        return jnp.logical_or(lower, upper)

    def shift(blk):
        return slope * (-blk * n * LOG2E)

    def tile_tops(blk, tk):
        tops = stat[blk * n_head + tk, 0:SUBS, :] + shift(blk)
        return jnp.where(seen_row(blk, tk), tops, -BIG)

    def combine(blks, tops, sums):
        top = tops
        for blk in blks:
            for tk in range(n_head):
                here = jnp.max(tile_tops(blk, tk), axis=0, keepdims=True)
                top = here if top is None else jnp.maximum(top, here)
        total = jnp.zeros((1, n), F32)
        for t, s in sums:
            total = total + s * jnp.exp2(t - top)
        for blk in blks:
            for tk in range(n_head):
                weight = jnp.exp2(tile_tops(blk, tk) - top)
                value = jnp.where(
                    seen_row(blk, tk), weight * stat[blk * n_head + tk, SUBS:2 * SUBS, :], 0.0
                )
                total = total + jnp.sum(value, axis=0, keepdims=True)
        return top, total

    def set_ratio(blk, lse):
        for tk in range(n_head):
            r = jnp.exp2(tile_tops(blk, tk) - lse)
            ratio[blk * n_head + tk, 0:SUBS, :] = jnp.where(seen_row(blk, tk), r, 0.0)

    def send_part(at, blks, by):
        top, total = combine(blks, None, ())
        part_out[at, 0:1, :] = top
        part_out[at, 1:2, :] = total
        send(part_out.at[at], part_in.at[at], s_ssem.at[at], s_rsem.at[at], along(by))

    def row_2(blk, tk, col, width, first_k, first_q, delta):
        qs, ks = QSLOT[blk], KSLOT[blk]
        cols = pl.ds(col, width)
        dp = lax.dot_general(
            vb[ks, rows(tk), :], gb[qs, cols, :], NT_DIMS, preferred_element_type=F32
        )
        delta_row = delta[:, cols]
        source = store_p(blk, tk, col, width)
        halves = []
        scores = []
        for u in range(SUBS):
            r = ratio[blk * n_head + tk, u:u + 1, cols].astype(BF16)
            half = source[u * sub:(u + 1) * sub, :] * r
            halves.append(half)
            scores.append(half * (dp[u * sub:(u + 1) * sub] - delta_row).astype(BF16))
        half = jnp.concatenate(halves, axis=0)
        score = jnp.concatenate(scores, axis=0)
        dv = jnp.dot(half, gb[qs, cols, :], preferred_element_type=F32)
        dk = jnp.dot(score, qx[qs, cols, 0:D], preferred_element_type=F32)
        dq = lax.dot_general(kx[ks, rows(tk), 0:D], score, TN_DIMS, preferred_element_type=F32)
        if first_k:
            dva[ks, rows(tk), :] = dv
            dka[ks, rows(tk), :] = dk
        else:
            dva[ks, rows(tk), :] += dv
            dka[ks, rows(tk), :] += dk
        if first_q:
            dqt[qs, :, cols] = dq
        else:
            dqt[qs, :, cols] += dq

    def send_dq(at, slot, by):
        for step in range(n_head):
            j = peer(step + 1)
            cols = pl.ds(pl.multiple_of(j * ch, ch), ch)
            dq_send[at, j, :, :] = dqt[slot, :, cols].astype(BF16)
            send(
                dq_send.at[at, j], dq_recv.at[at, j], dq_ssem.at[at, j], dq_rsem.at[at, j], along(by)
            )

    outs = (dq_out, dk_out, dv_out)

    def give(which, j):
        return remote(
            fin.at[which, j], outs[which].at[:, lanes(me)], o_ssem.at[which, j], o_rsem.at[which, me],
            (ctx, j),
        )

    def keep_out(which):
        return pltpu.make_async_copy(
            fin.at[which, me], outs[which].at[:, lanes(me)], o_rsem.at[which, me]
        )

    for by in order_in:
        j = peer(by)
        got_own(0, j)
        forward_rows(0, 0, j)
        got_own(1, j)
        forward_cols(1, 4, j)
    phase_1(A)
    for by in order_in:
        relay(0, 0, peer(by))
    for by in order_in:
        got_halo(1, 4, 1, peer(by))
    phase_1(DD)
    send_part(1, (DD,), 2)
    for by in order_in:
        j = peer(by)
        got_own(2, j)
        forward_rows(2, 2, j)
        got_own(3, j)
        forward_cols(3, 5, j)
    for by in order_in:
        got_halo(0, 1, 1, peer(by))
    phase_1(C)
    phase_1(B)
    send_part(0, (B, C), 1)
    for by in order_in:
        relay(2, 2, peer(by))
    for by in order_in:
        j = peer(by)
        arrived(delta_in.at[j], d_ssem.at[0], d_rsem.at[j])
    delta_own = jnp.concatenate([delta_in[j, 0:1, :] for j in range(n_head)], axis=1)
    for at in range(2):
        arrived(part_in.at[at], s_ssem.at[at], s_rsem.at[at])
    tops = [part_in[at, 0:1, :] for at in range(2)]
    sums = [(tops[at], part_in[at, 1:2, :]) for at in range(2)]
    top, total = combine((A,), jnp.maximum(tops[0], tops[1]), sums)
    lse = top + jnp.log(total) * LOG2E
    ret_out[0:1, :] = lse
    ret_out[1:2, :] = delta_own
    for at in range(2):
        send(ret_out, ret_in.at[at], s_ssem.at[2 + at], s_rsem.at[2 + at], along(-1 - at))
    set_ratio(A, lse)
    delta_a = ret_out.at[1:2, :]
    for tk in range(n_head):
        row_2(A, tk, tk * ch, n - tk * ch, True, tk == 0, delta_a)

    arrived(ret_in.at[1], s_ssem.at[3], s_rsem.at[3])
    set_ratio(DD, ret_in[1, 0:1, :])
    for by in order_in:
        got_halo(3, 5, 1, peer(by))
    delta_d = ret_in.at[1, 1:2, :]
    for tk in reversed(range(n_head)):
        row_2(DD, tk, 0, (tk + 1) * ch, True, tk == n_head - 1, delta_d)
    send_dq(1, 2, 2)

    arrived(ret_in.at[0], s_ssem.at[2], s_rsem.at[2])
    set_ratio(C, ret_in[0, 0:1, :])
    set_ratio(B, ret_in[0, 0:1, :])
    for by in order_in:
        got_halo(2, 3, 1, peer(by))
    delta_bc = ret_in.at[0, 1:2, :]
    dqt[1, :, :] = jnp.zeros((D, n), F32)

    def give_kv(which, j):
        return remote(
            dkv_send.at[which, j], dkv_recv.at[which, j], kv_ssem.at[which, j], kv_rsem.at[which, j],
            along(-1),
        )

    def step_c(step, _):
        tk = lax.rem(me + 1 + step, n_head)
        row_2(C, tk, 0, n, False, False, delta_bc)
        dkv_send[0, tk, :, :] = dka[1, rows(tk), :].astype(BF16)
        dkv_send[1, tk, :, :] = dva[1, rows(tk), :].astype(BF16)
        for which in range(2):
            give_kv(which, tk).start()
        return 0

    lax.fori_loop(0, n_head, step_c, 0)

    def step_b(step, _):
        tk = lax.rem(me + 1 + step, n_head)
        row_2(B, tk, 0, n, False, False, delta_bc)
        for which in range(2):
            give_kv(which, tk).wait_recv()
        dk = dka[0, rows(tk), :] + dkv_recv[0, tk, :, :].astype(F32)
        dv = dva[0, rows(tk), :] + dkv_recv[1, tk, :, :].astype(F32)
        fin[1, tk, :, :] = (dk * SCALE).astype(BF16)
        fin[2, tk, :, :] = dv.astype(BF16)

        @pl.when(step < n_head - 1)
        def _():
            give(1, tk).start()
            give(2, tk).start()

        return 0

    lax.fori_loop(0, n_head, step_b, 0)
    send_dq(0, 1, 1)
    keep_out(1).start()
    keep_out(2).start()
    for step in range(n_head):
        j = peer(step + 1)
        for at in (1, 0):
            arrived(dq_recv.at[at, j], dq_ssem.at[at, j], dq_rsem.at[at, j])
        cols = pl.ds(pl.multiple_of(j * ch, ch), ch)
        dq = dqt[0, :, cols] + dq_recv[0, j, :, :].astype(F32) + dq_recv[1, j, :, :].astype(F32)
        fin[0, j, :, :] = (dq.T * SCALE).astype(BF16)
        if step < n_head - 1:
            give(0, j).start()
    keep_out(0).start()

    for which in range(3):
        for step in range(n_head - 1):
            give(which, peer(step + 1)).wait_send()
    for which in range(2):
        for j in range(n_head):
            give_kv(which, j).wait_send()
    for copy in sends:
        copy.wait_send()
    for which in range(3):
        for step in range(n_head):
            j = peer(step)
            arrived(outs[which].at[:, lanes(j)], o_ssem.at[which, j], o_rsem.at[which, j])


def solution(mesh):
    n_ctx, n_head = mesh.shape["ctx"], mesh.shape["head"]

    def body(queries, keys, values, output, out_grad, slopes, windows):
        ch, width = queries.shape
        n = ch * n_head
        smem = pl.BlockSpec(memory_space=pltpu.SMEM)
        hbm = pl.BlockSpec(memory_space=pl.ANY)
        dma = pltpu.SemaphoreType.DMA
        vmem = pltpu.VMEM
        out = jax.ShapeDtypeStruct((ch, width), BF16)
        return pl.pallas_call(
            functools.partial(kernel, n_ctx, n_head),
            out_shape=[out] * 3,
            in_specs=[smem, smem] + [hbm] * 5,
            out_specs=[hbm] * 3,
            scratch_shapes=[
                vmem((3, n, 2 * D), BF16),
                vmem((2, n, 2 * D), BF16),
                vmem((3, n, D), BF16),
                vmem((2, n, D), BF16),
                vmem((ch, width), BF16),
                vmem((ch, width), BF16),
                vmem((n_head, ch, n + ch), BF16),
                vmem((n_head, ch, n), BF16),
                vmem((n_head, ch, n), BF16),
                vmem((4 * n_head, 2 * SUBS, n), F32),
                vmem((4 * n_head, SUBS, n), F32),
                vmem((3, D, n), F32),
                vmem((2, n, D), F32),
                vmem((2, n, D), F32),
                vmem((n_head, 8, ch), F32),
                vmem((n_head, 8, ch), F32),
                vmem((2, 8, n), F32),
                vmem((2, 8, n), F32),
                vmem((8, n), F32),
                vmem((2, 8, n), F32),
                vmem((2, n_head, D, ch), BF16),
                vmem((2, n_head, D, ch), BF16),
                vmem((2, n_head, ch, D), BF16),
                vmem((2, n_head, ch, D), BF16),
                vmem((3, n_head, ch, D), BF16),
                dma((4, n_head)),
                dma((4, n_head)),
                dma((6, n_head)),
                dma((6, n_head)),
                dma((n_head,)),
                dma((n_head,)),
                dma((4,)),
                dma((4,)),
                dma((2, n_head)),
                dma((2, n_head)),
                dma((2, n_head)),
                dma((2, n_head)),
                dma((3, n_head)),
                dma((3, n_head)),
                dma((2,)),
            ],
            compiler_params=pltpu.CompilerParams(
                collective_id=0, has_side_effects=True, vmem_limit_bytes=62 << 20
            ),
            cost_estimate=pl.CostEstimate(
                flops=2 * 5 * 3 * n * n * D, bytes_accessed=8 * ch * width * 2,
                transcendentals=3 * n * n,
            ),
        )(slopes, windows, queries, keys, values, output, out_grad)

    split = P(("ctx", "head"), None)
    return jax.shard_map(
        body,
        mesh=mesh,
        in_specs=(split,) * 5 + (P(), P()),
        out_specs=(split,) * 3,
        check_vma=False,
    )
```

profile of v0, /device:TPU:6, one launch (start us, length us, event | category | flops | bytes accessed | tf_op | source)
XLA Modules:
  0.0 96.0 jit_solution(14651927532468555514)
XLA Ops:
  0.6 91.4 %shard_map.94 = (bf16[512,512]{1,0:T(8,128)(2,1)}, bf16[512,512]{1,0:T(8,128)(2,1)}, bf16[512,512]{1,0:T(8,128)(2,1)}) custom-call(f32[4]{0:T(128)} %slopes.1, s32[4]{0:T(128)} %windows.1, bf16[512,512]{1,0:T(8,128)(2,1)} %q_in.1, bf16[512,512]{1,0:T(8,128)(2,1)} %k_in.1, bf16[512,512]{1,0:T(8,128)(2,1)} %v_in.1, bf16[512,512]{1,0:T(8,128)(2,1)} %o_in.1, ...), custom_call_target="tpu_custom_call" | custom-call | flops 16106127360 | bytes 4194304 | tf_op jit(solution)/shard_map/pallas_call | solution.py:502
  92.0 0.0 copy-start.1
  92.0 1.9 %copy.13 = bf16[512,512]{1,0:T(8,128)(2,1)} copy(bf16[512,512]{1,0:T(8,128)(2,1)} %get-tuple-element.6) | data formatting | bytes 1048576
  94.0 0.0 copy-done.1
  94.0 0.0 copy-start
  94.0 0.8 copy.14
  94.8 0.4 copy-done
  95.2 0.8 copy.15
Async XLA Ops:
  92.0 1.9 %copy-start.1 = (bf16[512,512]{1,0:T(8,128)(2,1)S(1)}, bf16[512,512]{1,0:T(8,128)(2,1)}, u32[]{:S(2)}) copy-start(bf16[512,512]{1,0:T(8,128)(2,1)} %get-tuple-element.7) | copy-start | bytes 1572868
  94.0 1.2 %copy-start = (bf16[512,512]{1,0:T(8,128)(2,1)S(1)}, bf16[512,512]{1,0:T(8,128)(2,1)}, u32[]{:S(2)}) copy-start(bf16[512,512]{1,0:T(8,128)(2,1)} %get-tuple-element.8) | copy-start | bytes 1572868
where the time goes:
time: 96.4 us; the launch traced here: 96 us
  Pallas kernels  91.4 us (95%)
  local copies, waits for them, and re-layouts  3.95 us (4%)
    pallas_call x1, Pallas kernels, body(): pl.pallas_call(functools.partial(kernel, n_ctx, n_head), out_shape=[out]...  91.4 us
    unnamed x7, local copies, waits for them, and re-layouts  3.95 us

commit v1 on v0

--- a/solution.py
+++ b/solution.py
@@ -58,6 +58,7 @@
     part_in,
     ret_out,
     ret_in,
+    deltas,
     dq_send,
     dq_recv,
     dkv_send,
@@ -143,10 +144,10 @@
         pl.semaphore_signal(barrier, inc=1, device_id=device, device_id_type=MESH)
     pl.semaphore_wait(barrier, len(neighbours))
 
-    for a in range(4):
-        for by in (1, 3, 2):
-            to = peer(by)
-            send(ins[a].at[:, lanes(to)], chunk(a, 0, me), x_ssem.at[a, by], x_rsem.at[a, me], (ctx, to))
+    first = ((0, 1), (0, 3), (1, 1), (1, 3), (0, 2), (1, 2))
+    for a, by in first + ((2, 1), (2, 3), (2, 2), (3, 1), (3, 3), (3, 2)):
+        to = peer(by)
+        send(ins[a].at[:, lanes(to)], chunk(a, 0, me), x_ssem.at[a, by], x_rsem.at[a, me], (ctx, to))
 
     lane = lax.broadcasted_iota(jnp.int32, (1, D), 1)
     ones = jnp.broadcast_to(jnp.where(lane < 3, 1.0, 0.0), (ch, D)).astype(BF16)
@@ -222,39 +223,36 @@
             kx[KSLOT[blk], rows(tk), :], qx[QSLOT[blk], pl.ds(col, ch), :], NT_DIMS,
             preferred_element_type=F32,
         )
-        if masked:
-            apart = lax.broadcasted_iota(jnp.int32, (ch, ch), 1) - lax.broadcasted_iota(
-                jnp.int32, (ch, ch), 0
-            )
-            seen = apart >= 0 if blk == A else apart < window - blk * n
-            s = jnp.where(seen, s, -BIG)
         target = store_p(blk, tk, col, ch)
         for u in range(SUBS):
-            part = s[u * sub:(u + 1) * sub] * TO_LOG2
+            part = s[u * sub:(u + 1) * sub]
+            if masked:
+                apart = lax.broadcasted_iota(jnp.int32, (sub, sub), 1) - lax.broadcasted_iota(
+                    jnp.int32, (sub, sub), 0
+                )
+                seen = apart >= 0 if blk == A else apart < window - blk * n
+                pieces = [jnp.where(seen, part[:, u * sub:(u + 1) * sub], -BIG)]
+                if u > 0:
+                    pieces.insert(0, part[:, :u * sub])
+                if u < SUBS - 1:
+                    pieces.append(part[:, (u + 1) * sub:])
+                part = jnp.concatenate(pieces, axis=1)
             top = jnp.max(part, axis=0, keepdims=True)
-            p = jnp.exp2(part - top)
+            p = jnp.exp2((part - top) * TO_LOG2)
             total = jnp.sum(p, axis=0, keepdims=True)
             target[u * sub:(u + 1) * sub, :] = p.astype(BF16)
-            stat[blk * n_head + tk, u:u + 1, pl.ds(col, ch)] = top
+            stat[blk * n_head + tk, u:u + 1, pl.ds(col, ch)] = top * TO_LOG2
             stat[blk * n_head + tk, SUBS + u:SUBS + u + 1, pl.ds(col, ch)] = total
 
-    def phase_1(blk):
-        if blk == A:
-            for tk in range(n_head):
-                for tq in range(tk, n_head):
+    half_n = n // 2
+    half_c = n_head // 2
+    halves_of = [pl.ds(h * half_n, half_n) for h in range(2)]
+
+    def phase_1(blk, h):
+        for tk in range(n_head):
+            for tq in range(h * half_c, (h + 1) * half_c):
+                if blk != DD or tq <= tk:
                     tile_1(blk, tk, tq * ch, tq == tk)
-        elif blk == DD:
-            for tk in range(n_head):
-                for tq in range(tk + 1):
-                    tile_1(blk, tk, tq * ch, tq == tk)
-        else:
-            def body(tk, _):
-                for u in range(n_head):
-                    tq = lax.rem(tk + u, n_head)
-                    tile_1(blk, tk, pl.multiple_of(tq * ch, ch), u == 0)
-                return 0
-
-            lax.fori_loop(0, n_head, body, 0)
 
     exists = (
         None,
@@ -262,61 +260,90 @@
         jnp.logical_and(ctx + 1 < n_ctx, ctx >= 1),
         jnp.logical_and(ctx + 2 < n_ctx, ctx >= 1),
     )
-    tq_lane = lax.broadcasted_iota(jnp.int32, (1, n), 1) // ch
-
-    def seen_row(blk, tk):
+    q_part = lax.broadcasted_iota(jnp.int32, (SUBS, half_n), 1) // sub
+    k_part = lax.broadcasted_iota(jnp.int32, (SUBS, half_n), 0)
+
+    def seen_row(blk, tk, h):
+        apart = q_part + h * half_c * SUBS - (k_part + tk * SUBS)
         if blk == A:
-            return tq_lane >= tk
+            return apart >= 0
         upto = jnp.where(exists[blk], window - blk * n, -1)
-        lower = jnp.logical_and(tq_lane <= tk, upto >= 0)
-        upper = jnp.logical_and(tq_lane > tk, upto > 0)
-        if blk == DD:
-            return lower
-        return jnp.logical_or(lower, upper)
+        return jnp.where(apart <= 0, upto, upto - 1) >= 0
 
     def shift(blk):
         return slope * (-blk * n * LOG2E)
 
-    def tile_tops(blk, tk):
-        tops = stat[blk * n_head + tk, 0:SUBS, :] + shift(blk)
-        return jnp.where(seen_row(blk, tk), tops, -BIG)
-
-    def combine(blks, tops, sums):
-        top = tops
+    def tile_tops(blk, tk, h):
+        tops = stat[blk * n_head + tk, 0:SUBS, halves_of[h]] + shift(blk)
+        return jnp.where(seen_row(blk, tk, h), tops, -BIG)
+
+    def tiles_in(blk, h):
+        if blk == A:
+            return range((h + 1) * half_c)
+        if blk == DD:
+            return range(h * half_c, n_head)
+        return range(n_head)
+
+    def combine(blks, h, parts):
+        tops = [tile_tops(blk, tk, h) for blk in blks for tk in tiles_in(blk, h)]
+        tall = functools.reduce(jnp.maximum, tops)
+        top = jnp.max(tall, axis=0, keepdims=True)
+        for t, _ in parts:
+            top = jnp.maximum(top, t)
+        total = jnp.zeros((1, half_n), F32)
+        for t, v in parts:
+            total = total + v * jnp.exp2(t - top)
+        several = jnp.zeros((SUBS, half_n), F32)
+        i = 0
         for blk in blks:
-            for tk in range(n_head):
-                here = jnp.max(tile_tops(blk, tk), axis=0, keepdims=True)
-                top = here if top is None else jnp.maximum(top, here)
-        total = jnp.zeros((1, n), F32)
-        for t, s in sums:
-            total = total + s * jnp.exp2(t - top)
+            for tk in tiles_in(blk, h):
+                sums = stat[blk * n_head + tk, SUBS:2 * SUBS, halves_of[h]]
+                several = several + jnp.where(
+                    seen_row(blk, tk, h), jnp.exp2(tops[i] - top) * sums, 0.0
+                )
+                i += 1
+        return top, total + jnp.sum(several, axis=0, keepdims=True)
+
+    def set_ratio(blk, h, lse):
+        for tk in tiles_in(blk, h):
+            r = jnp.exp2(tile_tops(blk, tk, h) - lse)
+            ratio[blk * n_head + tk, 0:SUBS, halves_of[h]] = jnp.where(seen_row(blk, tk, h), r, 0.0)
+
+    def send_part(at, h, blks):
+        top, total = combine(blks, h, ())
+        part_out[at, h, 0:1, :] = top
+        part_out[at, h, 1:2, :] = total
+        i = at * 2 + h
+        send(part_out.at[at, h], part_in.at[at, h], s_ssem.at[i], s_rsem.at[i], along(1 + at))
+
+    def send_lse(h):
+        for at in range(2):
+            i = at * 2 + h
+            arrived(part_in.at[at, h], s_ssem.at[i], s_rsem.at[i])
+        parts = [(part_in[at, h, 0:1, :], part_in[at, h, 1:2, :]) for at in range(2)]
+        top, total = combine((A,), h, parts)
+        lse = top + jnp.log(total) * LOG2E
+        ret_out[h, 0:1, :] = lse
+        ret_out[h, 1:2, :] = deltas[0:1, halves_of[h]]
+        for at in (1, 0):
+            i = 4 + at * 2 + h
+            send(ret_out.at[h], ret_in.at[at, h], s_ssem.at[i], s_rsem.at[i], along(-1 - at))
+        set_ratio(A, h, lse)
+
+    def got_lse(at, h, blks):
+        i = 4 + at * 2 + h
+        arrived(ret_in.at[at, h], s_ssem.at[i], s_rsem.at[i])
+        deltas[1 + at:2 + at, halves_of[h]] = ret_in[at, h, 1:2, :]
         for blk in blks:
-            for tk in range(n_head):
-                weight = jnp.exp2(tile_tops(blk, tk) - top)
-                value = jnp.where(
-                    seen_row(blk, tk), weight * stat[blk * n_head + tk, SUBS:2 * SUBS, :], 0.0
-                )
-                total = total + jnp.sum(value, axis=0, keepdims=True)
-        return top, total
-
-    def set_ratio(blk, lse):
-        for tk in range(n_head):
-            r = jnp.exp2(tile_tops(blk, tk) - lse)
-            ratio[blk * n_head + tk, 0:SUBS, :] = jnp.where(seen_row(blk, tk), r, 0.0)
-
-    def send_part(at, blks, by):
-        top, total = combine(blks, None, ())
-        part_out[at, 0:1, :] = top
-        part_out[at, 1:2, :] = total
-        send(part_out.at[at], part_in.at[at], s_ssem.at[at], s_rsem.at[at], along(by))
-
-    def row_2(blk, tk, col, width, first_k, first_q, delta):
+            set_ratio(blk, h, ret_in[at, h, 0:1, :])
+
+    def row_2(blk, tk, col, width, first_k, first_q):
         qs, ks = QSLOT[blk], KSLOT[blk]
         cols = pl.ds(col, width)
         dp = lax.dot_general(
             vb[ks, rows(tk), :], gb[qs, cols, :], NT_DIMS, preferred_element_type=F32
         )
-        delta_row = delta[:, cols]
+        delta_row = deltas[qs:qs + 1, cols]
         source = store_p(blk, tk, col, width)
         halves = []
         scores = []
@@ -363,67 +390,89 @@
             fin.at[which, me], outs[which].at[:, lanes(me)], o_rsem.at[which, me]
         )
 
+    near = [peer(by) for by in range(n_head)]
+
+    def rows_on(a, row, bys):
+        for by in bys:
+            got_own(a, near[by])
+            forward_rows(a, row, near[by])
+
+    def cols_on(a, row, bys):
+        for by in bys:
+            got_own(a, near[by])
+            forward_cols(a, row, near[by])
+
+    here = []
+
+    def tiles_of(by):
+        j = near[by]
+        tile_1(A, j, pl.multiple_of(j * ch, ch), True)
+        for other in here:
+            tk, tq = jnp.minimum(other, j), jnp.maximum(other, j)
+            tile_1(A, tk, pl.multiple_of(tq * ch, ch), False)
+        here.append(j)
+
+    rows_on(0, 0, (0,))
+    cols_on(1, 4, (0,))
+    tiles_of(0)
+    rows_on(0, 0, (1, 3))
+    cols_on(1, 4, (1, 3))
+    tiles_of(1)
+    tiles_of(3)
+    rows_on(0, 0, (2,))
+    cols_on(1, 4, (2,))
+    rows_on(2, 2, (0,))
+    cols_on(3, 5, (0,))
+    tiles_of(2)
     for by in order_in:
-        j = peer(by)
-        got_own(0, j)
-        forward_rows(0, 0, j)
-        got_own(1, j)
-        forward_cols(1, 4, j)
-    phase_1(A)
+        relay(0, 0, near[by])
     for by in order_in:
-        relay(0, 0, peer(by))
+        got_halo(1, 4, 1, near[by])
+    phase_1(DD, 0)
+    rows_on(2, 2, (1, 3))
     for by in order_in:
-        got_halo(1, 4, 1, peer(by))
-    phase_1(DD)
-    send_part(1, (DD,), 2)
+        got_halo(0, 1, 1, near[by])
+    phase_1(C, 0)
+    rows_on(2, 2, (2,))
+    send_part(1, 0, (DD,))
+    phase_1(B, 0)
+    send_part(0, 0, (B, C))
+    cols_on(3, 5, (1, 3))
+    phase_1(DD, 1)
+    send_part(1, 1, (DD,))
+    phase_1(C, 1)
+    cols_on(3, 5, (2,))
+    for j in near:
+        arrived(delta_in.at[j], d_ssem.at[0], d_rsem.at[j])
+    deltas[0:1, :] = jnp.concatenate([delta_in[j, 0:1, :] for j in range(n_head)], axis=1)
+    send_lse(0)
+    phase_1(B, 1)
+    send_part(0, 1, (B, C))
     for by in order_in:
-        j = peer(by)
-        got_own(2, j)
-        forward_rows(2, 2, j)
-        got_own(3, j)
-        forward_cols(3, 5, j)
+        relay(2, 2, near[by])
+    for slot in range(2):
+        dqt[slot, :, :] = jnp.zeros((D, n), F32)
+
+    got_lse(1, 0, (DD,))
     for by in order_in:
-        got_halo(0, 1, 1, peer(by))
-    phase_1(C)
-    phase_1(B)
-    send_part(0, (B, C), 1)
+        got_halo(3, 5, 1, near[by])
+    for tk in reversed(range(n_head)):
+        row_2(DD, tk, 0, min(tk + 1, half_c) * ch, True, tk == n_head - 1)
+    send_lse(1)
+    got_lse(0, 0, (B, C))
     for by in order_in:
-        relay(2, 2, peer(by))
-    for by in order_in:
-        j = peer(by)
-        arrived(delta_in.at[j], d_ssem.at[0], d_rsem.at[j])
-    delta_own = jnp.concatenate([delta_in[j, 0:1, :] for j in range(n_head)], axis=1)
-    for at in range(2):
-        arrived(part_in.at[at], s_ssem.at[at], s_rsem.at[at])
-    tops = [part_in[at, 0:1, :] for at in range(2)]
-    sums = [(tops[at], part_in[at, 1:2, :]) for at in range(2)]
-    top, total = combine((A,), jnp.maximum(tops[0], tops[1]), sums)
-    lse = top + jnp.log(total) * LOG2E
-    ret_out[0:1, :] = lse
-    ret_out[1:2, :] = delta_own
-    for at in range(2):
-        send(ret_out, ret_in.at[at], s_ssem.at[2 + at], s_rsem.at[2 + at], along(-1 - at))
-    set_ratio(A, lse)
-    delta_a = ret_out.at[1:2, :]
-    for tk in range(n_head):
-        row_2(A, tk, tk * ch, n - tk * ch, True, tk == 0, delta_a)
-
-    arrived(ret_in.at[1], s_ssem.at[3], s_rsem.at[3])
-    set_ratio(DD, ret_in[1, 0:1, :])
-    for by in order_in:
-        got_halo(3, 5, 1, peer(by))
-    delta_d = ret_in.at[1, 1:2, :]
-    for tk in reversed(range(n_head)):
-        row_2(DD, tk, 0, (tk + 1) * ch, True, tk == n_head - 1, delta_d)
+        got_halo(2, 3, 1, near[by])
+
+    def first_c(tk, _):
+        row_2(C, tk, 0, half_n, False, False)
+        return 0
+
+    lax.fori_loop(0, n_head, first_c, 0)
+    got_lse(1, 1, (DD,))
+    for tk in reversed(range(half_c, n_head)):
+        row_2(DD, tk, half_n, (tk + 1 - half_c) * ch, False, tk == n_head - 1)
     send_dq(1, 2, 2)
-
-    arrived(ret_in.at[0], s_ssem.at[2], s_rsem.at[2])
-    set_ratio(C, ret_in[0, 0:1, :])
-    set_ratio(B, ret_in[0, 0:1, :])
-    for by in order_in:
-        got_halo(2, 3, 1, peer(by))
-    delta_bc = ret_in.at[0, 1:2, :]
-    dqt[1, :, :] = jnp.zeros((D, n), F32)
+    got_lse(0, 1, (B, C))
 
     def give_kv(which, j):
         return remote(
@@ -431,9 +480,14 @@
             along(-1),
         )
 
+    def give_dq(at, j, by):
+        return remote(
+            dq_send.at[at, j], dq_recv.at[at, j], dq_ssem.at[at, j], dq_rsem.at[at, j], along(by)
+        )
+
     def step_c(step, _):
         tk = lax.rem(me + 1 + step, n_head)
-        row_2(C, tk, 0, n, False, False, delta_bc)
+        row_2(C, tk, half_n, half_n, False, False)
         dkv_send[0, tk, :, :] = dka[1, rows(tk), :].astype(BF16)
         dkv_send[1, tk, :, :] = dva[1, rows(tk), :].astype(BF16)
         for which in range(2):
@@ -442,9 +496,30 @@
 
     lax.fori_loop(0, n_head, step_c, 0)
 
-    def step_b(step, _):
+    def step_ab(step, _):
         tk = lax.rem(me + 1 + step, n_head)
-        row_2(B, tk, 0, n, False, False, delta_bc)
+        for at in range(n_head):
+
+            @pl.when(tk == at)
+            def _():
+                row_2(A, at, at * ch, n - at * ch, True, False)
+
+        @pl.when(step < n_head - 1)
+        def _():
+            row_2(B, tk, 0, n, False, False)
+
+        @pl.when(step == n_head - 1)
+        def _():
+            def tile(i, _):
+                tq = lax.rem(me + 1 + i, n_head)
+                cols = pl.ds(pl.multiple_of(tq * ch, ch), ch)
+                row_2(B, tk, pl.multiple_of(tq * ch, ch), ch, False, False)
+                dq_send[0, tq, :, :] = dqt[1, :, cols].astype(BF16)
+                give_dq(0, tq, 1).start()
+                return 0
+
+            lax.fori_loop(0, n_head, tile, 0)
+
         for which in range(2):
             give_kv(which, tk).wait_recv()
         dk = dka[0, rows(tk), :] + dkv_recv[0, tk, :, :].astype(F32)
@@ -459,8 +534,7 @@
 
         return 0
 
-    lax.fori_loop(0, n_head, step_b, 0)
-    send_dq(0, 1, 1)
+    lax.fori_loop(0, n_head, step_ab, 0)
     keep_out(1).start()
     keep_out(2).start()
     for step in range(n_head):
@@ -474,6 +548,8 @@
             give(0, j).start()
     keep_out(0).start()
 
+    for j in range(n_head):
+        give_dq(0, j, 1).wait_send()
     for which in range(3):
         for step in range(n_head - 1):
             give(which, peer(step + 1)).wait_send()
@@ -488,6 +564,27 @@
             arrived(outs[which].at[:, lanes(j)], o_ssem.at[which, j], o_rsem.at[which, j])
 
 
+def copy_out(*refs):
+    ins, outs, buf, sems = refs[:3], refs[3:6], refs[6], refs[7]
+    parts = sems.shape[2]
+    step = ins[0].shape[0] // parts
+    moves = []
+    for i in range(3):
+        for j in range(parts):
+            at = pl.ds(j * step, step)
+            moves.append((
+                pltpu.make_async_copy(ins[i].at[at], buf.at[i, at], sems.at[0, i, j]),
+                pltpu.make_async_copy(buf.at[i, at], outs[i].at[at], sems.at[1, i, j]),
+            ))
+    for load, _ in moves:
+        load.start()
+    for load, store in moves:
+        load.wait()
+        store.start()
+    for _, store in moves:
+        store.wait()
+
+
 def solution(mesh):
     n_ctx, n_head = mesh.shape["ctx"], mesh.shape["head"]
 
@@ -499,7 +596,7 @@
         dma = pltpu.SemaphoreType.DMA
         vmem = pltpu.VMEM
         out = jax.ShapeDtypeStruct((ch, width), BF16)
-        return pl.pallas_call(
+        grads = pl.pallas_call(
             functools.partial(kernel, n_ctx, n_head),
             out_shape=[out] * 3,
             in_specs=[smem, smem] + [hbm] * 5,
@@ -521,10 +618,11 @@
                 vmem((2, n, D), F32),
                 vmem((n_head, 8, ch), F32),
                 vmem((n_head, 8, ch), F32),
-                vmem((2, 8, n), F32),
-                vmem((2, 8, n), F32),
-                vmem((8, n), F32),
-                vmem((2, 8, n), F32),
+                vmem((2, 2, 2, n // 2), F32),
+                vmem((2, 2, 2, n // 2), F32),
+                vmem((2, 2, n // 2), F32),
+                vmem((2, 2, 2, n // 2), F32),
+                vmem((3, n), F32),
                 vmem((2, n_head, D, ch), BF16),
                 vmem((2, n_head, D, ch), BF16),
                 vmem((2, n_head, ch, D), BF16),
@@ -536,8 +634,8 @@
                 dma((6, n_head)),
                 dma((n_head,)),
                 dma((n_head,)),
-                dma((4,)),
-                dma((4,)),
+                dma((8,)),
+                dma((8,)),
                 dma((2, n_head)),
                 dma((2, n_head)),
                 dma((2, n_head)),
@@ -554,6 +652,13 @@
                 transcendentals=3 * n * n,
             ),
         )(slopes, windows, queries, keys, values, output, out_grad)
+        return pl.pallas_call(
+            copy_out,
+            out_shape=[out] * 3,
+            in_specs=[hbm] * 3,
+            out_specs=[hbm] * 3,
+            scratch_shapes=[vmem((3, ch, width), BF16), dma((2, 3, 2))],
+        )(*grads)
 
     split = P(("ctx", "head"), None)
     return jax.shard_map(

time: 96.4 us -> 89.2 us (0.925)
  local copies, waits for them, and re-layouts: 3.95 us -> 0 us
  Pallas kernels: 91.4 us -> 88 us
    pallas_call x1, Pallas kernels: 91.4 us -> 85.8 us  [body(): pl.pallas_call(functools.partial(kernel, n_ctx, n_head), out_shape=[out]...]
    unnamed x7 -> x0, local copies, waits for them, and re-layouts: 3.95 us -> none
    pallas_call x0 -> x1, Pallas kernels: none -> 2.19 us  [body(): pl.pallas_call(copy_out, out_shape=[out] * 3, in_specs=[hbm] * 3, out_spe...]
where the time goes in v1:
time: 89.2 us; the launch traced here: 88.8 us
  Pallas kernels  88 us (99%)
    pallas_call x1, Pallas kernels, body(): pl.pallas_call(functools.partial(kernel, n_ctx, n_head), out_shape=[out]...  85.8 us
    pallas_call x1, Pallas kernels, body(): pl.pallas_call(copy_out, out_shape=[out] * 3, in_specs=[hbm] * 3, out_spe...  2.19 us

profile of v1, /device:TPU:6, one launch (start us, length us, event | category | flops | bytes accessed | tf_op | source)
XLA Modules:
  0.0 88.8 jit_solution(166266885352915881)
XLA Ops:
  0.6 85.8 %shard_map.94 = (bf16[512,512]{1,0:T(8,128)(2,1)}, bf16[512,512]{1,0:T(8,128)(2,1)}, bf16[512,512]{1,0:T(8,128)(2,1)}) custom-call(f32[4]{0:T(128)} %slopes.1, s32[4]{0:T(128)} %windows.1, bf16[512,512]{1,0:T(8,128)(2,1)} %q_in.1, bf16[512,512]{1,0:T(8,128)(2,1)} %k_in.1, bf16[512,512]{1,0:T(8,128)(2,1)} %v_in.1, bf16[512,512]{1,0:T(8,128)(2,1)} %o_in.1, ...), custom_call_target="tpu_custom_call" | custom-call | flops 16106127360 | bytes 4194304 | tf_op jit(solution)/shard_map/pallas_call | solution.py:599
  86.5 2.2 %shard_map.95 = (bf16[512,512]{1,0:T(8,128)(2,1)}, bf16[512,512]{1,0:T(8,128)(2,1)}, bf16[512,512]{1,0:T(8,128)(2,1)}) custom-call(bf16[512,512]{1,0:T(8,128)(2,1)} %get-tuple-element.6.refs_0_, bf16[512,512]{1,0:T(8,128)(2,1)} %get-tuple-element.7.refs_1_, bf16[512,512]{1,0:T(8,128)(2,1)} %get-tuple-element.8.refs_2_), custom_call_target="tpu_custom_call" | custom-call | tf_op jit(solution)/shard_map/pallas_call | solution.py:655

commit v2 on v1

--- a/solution.py
+++ b/solution.py
@@ -167,6 +167,9 @@
 
     lax.fori_loop(0, n_head, fill, 0)
 
+    for slot in range(2):
+        dqt[slot, :, :] = jnp.zeros((D, n), F32)
+
     copy_o.wait()
     copy_g.wait()
     for h in range(n_head):
@@ -450,29 +453,22 @@
     send_part(0, 1, (B, C))
     for by in order_in:
         relay(2, 2, near[by])
-    for slot in range(2):
-        dqt[slot, :, :] = jnp.zeros((D, n), F32)
-
+    for tk in range(half_c):
+        row_2(A, tk, tk * ch, half_n - tk * ch, True, False)
+    send_lse(1)
     got_lse(1, 0, (DD,))
     for by in order_in:
         got_halo(3, 5, 1, near[by])
     for tk in reversed(range(n_head)):
         row_2(DD, tk, 0, min(tk + 1, half_c) * ch, True, tk == n_head - 1)
-    send_lse(1)
-    got_lse(0, 0, (B, C))
-    for by in order_in:
-        got_halo(2, 3, 1, near[by])
-
-    def first_c(tk, _):
-        row_2(C, tk, 0, half_n, False, False)
-        return 0
-
-    lax.fori_loop(0, n_head, first_c, 0)
     got_lse(1, 1, (DD,))
     for tk in reversed(range(half_c, n_head)):
         row_2(DD, tk, half_n, (tk + 1 - half_c) * ch, False, tk == n_head - 1)
     send_dq(1, 2, 2)
+    got_lse(0, 0, (B, C))
     got_lse(0, 1, (B, C))
+    for by in order_in:
+        got_halo(2, 3, 1, near[by])
 
     def give_kv(which, j):
         return remote(
@@ -487,7 +483,7 @@
 
     def step_c(step, _):
         tk = lax.rem(me + 1 + step, n_head)
-        row_2(C, tk, half_n, half_n, False, False)
+        row_2(C, tk, 0, n, False, False)
         dkv_send[0, tk, :, :] = dka[1, rows(tk), :].astype(BF16)
         dkv_send[1, tk, :, :] = dva[1, rows(tk), :].astype(BF16)
         for which in range(2):
@@ -502,7 +498,8 @@
 
             @pl.when(tk == at)
             def _():
-                row_2(A, at, at * ch, n - at * ch, True, False)
+                start = max(at * ch, half_n)
+                row_2(A, at, start, n - start, at >= half_c, False)
 
         @pl.when(step < n_head - 1)
         def _():

time: 89.2 us -> 88.1 us (0.988)
  Pallas kernels: 88 us -> 87.1 us
    pallas_call x1, Pallas kernels: 85.8 us -> 84.9 us  [body(): pl.pallas_call(functools.partial(kernel, n_ctx, n_head), out_shape=[out]...]
where the time goes in v2:
time: 88.1 us; the launch traced here: 87.9 us
  Pallas kernels  87.1 us (99%)
    pallas_call x1, Pallas kernels, body(): pl.pallas_call(functools.partial(kernel, n_ctx, n_head), out_shape=[out]...  84.9 us
    pallas_call x1, Pallas kernels, body(): pl.pallas_call(copy_out, out_shape=[out] * 3, in_specs=[hbm] * 3, out_spe...  2.19 us

profile of v2, /device:TPU:6, one launch (start us, length us, event | category | flops | bytes accessed | tf_op | source)
XLA Modules:
  0.0 87.9 jit_solution(17827396724337680474)
XLA Ops:
  0.6 84.9 %shard_map.94 = (bf16[512,512]{1,0:T(8,128)(2,1)}, bf16[512,512]{1,0:T(8,128)(2,1)}, bf16[512,512]{1,0:T(8,128)(2,1)}) custom-call(f32[4]{0:T(128)} %slopes.1, s32[4]{0:T(128)} %windows.1, bf16[512,512]{1,0:T(8,128)(2,1)} %q_in.1, bf16[512,512]{1,0:T(8,128)(2,1)} %k_in.1, bf16[512,512]{1,0:T(8,128)(2,1)} %v_in.1, bf16[512,512]{1,0:T(8,128)(2,1)} %o_in.1, ...), custom_call_target="tpu_custom_call" | custom-call | flops 16106127360 | bytes 4194304 | tf_op jit(solution)/shard_map/pallas_call | solution.py:596
  85.6 2.2 %shard_map.95 = (bf16[512,512]{1,0:T(8,128)(2,1)}, bf16[512,512]{1,0:T(8,128)(2,1)}, bf16[512,512]{1,0:T(8,128)(2,1)}) custom-call(bf16[512,512]{1,0:T(8,128)(2,1)} %get-tuple-element.6.refs_0_, bf16[512,512]{1,0:T(8,128)(2,1)} %get-tuple-element.7.refs_1_, bf16[512,512]{1,0:T(8,128)(2,1)} %get-tuple-element.8.refs_2_), custom_call_target="tpu_custom_call" | custom-call | tf_op jit(solution)/shard_map/pallas_call | solution.py:652

commit v3 on v2

--- a/solution.py
+++ b/solution.py
@@ -492,6 +492,14 @@
 
     lax.fori_loop(0, n_head, step_c, 0)
 
+    def finish_kv(tk):
+        for which in range(2):
+            give_kv(which, tk).wait_recv()
+        dk = dka[0, rows(tk), :] + dkv_recv[0, tk, :, :].astype(F32)
+        dv = dva[0, rows(tk), :] + dkv_recv[1, tk, :, :].astype(F32)
+        fin[1, tk, :, :] = (dk * SCALE).astype(BF16)
+        fin[2, tk, :, :] = dv.astype(BF16)
+
     def step_ab(step, _):
         tk = lax.rem(me + 1 + step, n_head)
         for at in range(n_head):
@@ -517,23 +525,15 @@
 
             lax.fori_loop(0, n_head, tile, 0)
 
-        for which in range(2):
-            give_kv(which, tk).wait_recv()
-        dk = dka[0, rows(tk), :] + dkv_recv[0, tk, :, :].astype(F32)
-        dv = dva[0, rows(tk), :] + dkv_recv[1, tk, :, :].astype(F32)
-        fin[1, tk, :, :] = (dk * SCALE).astype(BF16)
-        fin[2, tk, :, :] = dv.astype(BF16)
-
         @pl.when(step < n_head - 1)
         def _():
+            finish_kv(tk)
             give(1, tk).start()
             give(2, tk).start()
 
         return 0
 
     lax.fori_loop(0, n_head, step_ab, 0)
-    keep_out(1).start()
-    keep_out(2).start()
     for step in range(n_head):
         j = peer(step + 1)
         for at in (1, 0):
@@ -544,6 +544,9 @@
         if step < n_head - 1:
             give(0, j).start()
     keep_out(0).start()
+    finish_kv(me)
+    keep_out(1).start()
+    keep_out(2).start()
 
     for j in range(n_head):
         give_dq(0, j, 1).wait_send()

time: 88.1 us -> 88.1 us (level)
  no operation moved by 1% of the time
where the time goes in v3:
time: 88.1 us; the launch traced here: 87.9 us
  Pallas kernels  87.1 us (99%)
    pallas_call x1, Pallas kernels, body(): pl.pallas_call(functools.partial(kernel, n_ctx, n_head), out_shape=[out]...  84.9 us
    pallas_call x1, Pallas kernels, body(): pl.pallas_call(copy_out, out_shape=[out] * 3, in_specs=[hbm] * 3, out_spe...  2.19 us

profile of v3, /device:TPU:6, one launch (start us, length us, event | category | flops | bytes accessed | tf_op | source)
XLA Modules:
  0.0 87.9 jit_solution(11402852039512516925)
XLA Ops:
  0.6 84.9 %shard_map.94 = (bf16[512,512]{1,0:T(8,128)(2,1)}, bf16[512,512]{1,0:T(8,128)(2,1)}, bf16[512,512]{1,0:T(8,128)(2,1)}) custom-call(f32[4]{0:T(128)} %slopes.1, s32[4]{0:T(128)} %windows.1, bf16[512,512]{1,0:T(8,128)(2,1)} %q_in.1, bf16[512,512]{1,0:T(8,128)(2,1)} %k_in.1, bf16[512,512]{1,0:T(8,128)(2,1)} %v_in.1, bf16[512,512]{1,0:T(8,128)(2,1)} %o_in.1, ...), custom_call_target="tpu_custom_call" | custom-call | flops 16106127360 | bytes 4194304 | tf_op jit(solution)/shard_map/pallas_call | solution.py:599
  85.5 2.2 %shard_map.95 = (bf16[512,512]{1,0:T(8,128)(2,1)}, bf16[512,512]{1,0:T(8,128)(2,1)}, bf16[512,512]{1,0:T(8,128)(2,1)}) custom-call(bf16[512,512]{1,0:T(8,128)(2,1)} %get-tuple-element.6.refs_0_, bf16[512,512]{1,0:T(8,128)(2,1)} %get-tuple-element.7.refs_1_, bf16[512,512]{1,0:T(8,128)(2,1)} %get-tuple-element.8.refs_2_), custom_call_target="tpu_custom_call" | custom-call | tf_op jit(solution)/shard_map/pallas_call | solution.py:655
